TPU v7x, 32 devices: a whole 2x2x4 slice. The times are simulated.
32 devices in a mesh: groups: 2 (over y), replica: 4 (over z), tensor: 2 (over x), section: 2 (over core).
Axes of the slice: x: 2, y: 2, z: 4, core: 2. Of those that a mesh axis runs over, the one named last changes fastest.
Arguments:
- queries: bfloat16 [8, 2, 64, 128, 128], P(('groups', 'replica'), 'section', 'tensor'), parts along dimension 0, may hold values from -0.52734375 to 0.52734375
- key_rows: bfloat16 [8, 2, 64, 128, 128], P(('groups', 'replica'), 'section', 'tensor'), parts along dimension 0, may hold values from -6 to 6
- value_rows: bfloat16 [8, 2, 64, 128, 128], P(('groups', 'replica'), 'section', 'tensor'), parts along dimension 0, may hold values from -6 to 6
- state_in: float32 [8, 2, 64, 128, 128], P(('groups', 'replica'), 'section', 'tensor'), parts along dimension 0, may hold values from -12 to 12
- lengths: int32 [8], P('groups'), parts along dimension 0, may hold values from 1 to 128, as said below
- assignment: int32 [8, 2, 64], P('groups'), parts along dimension 0, may hold values from 0 to 3, as said below
- head_rate: int32 [2, 64], P('section', 'tensor'), may hold values from 0 to 63
- decay_table: float32 [64], replicated, may hold values from 0.001953125 to 0.0390625
Outputs:
- helper_out: bfloat16 [8, 2, 64, 128, 128], P(('groups', 'replica'), 'section', 'tensor'), parts along dimension 0
- state_out: float32 [8, 2, 64, 128, 128], P(('groups', 'replica'), 'section', 'tensor'), parts along dimension 0
There are 2 independent parts, one for each index of `groups`. A program takes and returns all parts, laid end to end along the dimension named above; an argument that names none is the same for every part. Nothing has to cross between parts.
Inputs may be any that keep to these rules, and one draw needn't show every extreme that they name: `assignment`: for each layer and tensor block of 32 heads: one replica's block names each replica at most 8 times, some pair reaches 8, and every replica is named exactly 32 times over all replicas. `lengths`: some replica's block is full.
All inputs are finite; a program needn't handle non-finite values.
Results may differ from a plain program's by a relative error of at most 0.0048.
Values may be sent and summed in bfloat16 or wider, within the bound.
A program may use at most 64 MiB of HBM per device.

v0:
```python
import jax
import jax.numpy as jnp
from jax import lax
from jax.sharding import PartitionSpec as P


def inter_part(query_rows, state, rate):
    steps = jnp.arange(query_rows.shape[1]).astype(jnp.float32) + 1.0
    powers = jnp.exp(-rate[:, None] * steps[None, :])
    mixed = jnp.einsum(
        "bld,bde->ble", query_rows.astype(jnp.float32), state, precision=lax.Precision.HIGHEST
    )
    return powers[:, :, None] * mixed


def intra_part(query_rows, key_block, value_block, rate):
    positions = jnp.arange(query_rows.shape[1])
    gaps = (positions[:, None] - positions[None, :]).astype(jnp.float32)
    causal = positions[:, None] >= positions[None, :]
    scores = jnp.einsum("bid,bjd->bij", query_rows, key_block, preferred_element_type=jnp.float32)
    weight = jnp.where(
        causal[None], jnp.exp(-rate[:, None, None] * jnp.maximum(gaps, 0.0)[None]), 0.0
    )
    probs = (scores * weight).astype(jnp.bfloat16)
    return jnp.einsum("bij,bjd->bid", probs, value_block, preferred_element_type=jnp.float32)


def delta_part(key_block, value_block, rate, counts):
    positions = jnp.arange(key_block.shape[1])
    filled = positions[None, :] < counts[:, None]
    remain = (counts[:, None] - 1 - positions[None, :]).astype(jnp.float32)
    weight = jnp.where(filled, jnp.exp(-rate[:, None] * jnp.maximum(remain, 0.0)), 0.0)
    scaled = key_block.astype(jnp.float32) * weight[:, :, None]
    return jnp.einsum(
        "bjd,bje->bde", scaled, value_block.astype(jnp.float32), precision=lax.Precision.HIGHEST
    )


def finish_rows(intra, inter, counts):
    positions = jnp.arange(intra.shape[1])
    filled = positions[None, :] < counts[:, None]
    return jnp.where(filled[:, :, None], intra + inter, 0.0).astype(jnp.bfloat16)


def end_state(state, delta, rate, counts):
    return jnp.exp(-rate * counts.astype(jnp.float32))[:, None, None] * state + delta


def block_ranks(targets):
    order = jnp.arange(targets.shape[-1])
    same = targets[..., :, None] == targets[..., None, :]
    earlier = order[None, :] < order[:, None]
    return jnp.sum(same & earlier, axis=-1)


def compute_items(query_rows, key_block, value_block, state_rows, decay_rows, count_rows):
    inter = inter_part(query_rows, state_rows, decay_rows)
    intra = intra_part(query_rows, key_block, value_block, decay_rows)
    delta = delta_part(key_block, value_block, decay_rows, count_rows)
    return (
        finish_rows(intra, inter, count_rows),
        end_state(state_rows, delta, decay_rows, count_rows),
    )


def local(queries, key_rows, value_rows, state_in, lengths, assignment, head_rate, decay_table):
    query_rows = queries[0, 0]
    key_block = key_rows[0, 0]
    value_block = value_rows[0, 0]
    held_state = state_in[0, 0]
    heads_dev = query_rows.shape[0]
    token_slots = query_rows.shape[1]
    head_size = query_rows.shape[2]
    replicas = lax.axis_size("replica")
    per_pair = max(1, heads_dev // replicas)
    slot_total = replicas * per_pair
    myself = lax.axis_index("replica")
    my_layer = lax.axis_index("section")
    my_block = lax.axis_index("tensor")
    targets = lax.dynamic_slice(
        assignment, (jnp.int32(0), my_layer, my_block * heads_dev), (replicas, 1, heads_dev)
    )[:, 0, :]
    ranks = block_ranks(targets)
    picks = head_rate[0][:, None] == jnp.arange(decay_table.shape[0])[None, :]
    head_decay = jnp.sum(jnp.where(picks, decay_table[None, :], 0.0), axis=1)
    own_target = lax.dynamic_index_in_dim(targets, myself, 0, keepdims=False)
    own_rank = lax.dynamic_index_in_dim(ranks, myself, 0, keepdims=False)
    position = own_target * per_pair + own_rank
    own_counts = jnp.full((heads_dev,), lengths[myself], jnp.int32)
    matches = (targets[:, None, :] == myself) & (
        ranks[:, None, :] == jnp.arange(per_pair)[None, :, None]
    )
    matches = matches.reshape(slot_total, heads_dev)
    occupied = jnp.any(matches, axis=1)
    chosen = jnp.nonzero(occupied, size=heads_dev, fill_value=0)[0]
    state_send = (
        jnp.zeros((slot_total, head_size, head_size), jnp.float32).at[chosen].set(held_state)
    )
    state_home = lax.all_to_all(state_send, "replica", split_axis=0, concat_axis=0, tiled=True)
    carried = state_home[position]
    result, final = compute_items(
        query_rows, key_block, value_block, carried, head_decay, own_counts
    )
    rows_send = (
        jnp.zeros((slot_total, token_slots, head_size), jnp.bfloat16).at[position].set(result)
    )
    finals_send = jnp.zeros((slot_total, head_size, head_size), jnp.float32).at[position].set(final)
    rows_back, finals_back = (
        lax.all_to_all(
            rows_send.astype(jnp.float32), "replica", split_axis=0, concat_axis=0, tiled=True
        ).astype(rows_send.dtype),
        lax.all_to_all(finals_send, "replica", split_axis=0, concat_axis=0, tiled=True),
    )
    helper_rows = rows_back[chosen]
    final_states = finals_back[chosen]
    return (helper_rows[None, None], final_states[None, None])


def solution(mesh):
    in_specs = (
        P(("groups", "replica"), "section", "tensor", None, None),
        P(("groups", "replica"), "section", "tensor", None, None),
        P(("groups", "replica"), "section", "tensor", None, None),
        P(("groups", "replica"), "section", "tensor", None, None),
        P("groups"),
        P("groups", None, None),
        P("section", "tensor"),
        P(),
    )
    out_specs = (
        P(("groups", "replica"), "section", "tensor", None, None),
        P(("groups", "replica"), "section", "tensor", None, None),
    )
    return jax.shard_map(local, mesh=mesh, in_specs=in_specs, out_specs=out_specs, check_vma=False)
```

profile of v0, /device:TPU:0, one launch (start us, length us, event | category | flops | bytes accessed | tf_op | source)
XLA Modules:
  0.0 164.9 jit_solution(14472483725102810975)
XLA Ops:
  0.7 0.9 broadcast_compare_fusion
  2.9 0.8 scatter_custom_fusion
  3.8 0.8 fusion.25
  4.6 1.6 broadcast_in_dim.53.clone.2
  6.1 5.3 %scatter_fusion = f32[32,128,128]{2,1,0:T(8,128)} fusion(f32[32,128,128]{2,1,0:T(8,128)} %broadcast_in_dim.53.clone.2, s32[32]{0:T(128)S(1)} %fusion.25, f32[32,128,128]{2,1,0:T(8,128)S(1)} %bitcast.40), kind=kCustom, calls=%fused_computation.4 | custom fusion | bytes 6291584 | tf_op jit(solution)/shard_map/scatter | solution.py:97
  11.5 6.4 %all-to-all-start = ((f32[32,128,128]{2,1,0:T(8,128)}), f32[32,128,128]{2,1,0:T(8,128)}, u32[]{:S(2)}, u32[]{:S(2)}) async-start(f32[32,128,128]{2,1,0:T(8,128)} %scatter_fusion), calls=%async_computation | async-start | bytes 4194304 | tf_op jit(solution)/shard_map/all_to_all | solution.py:99
  17.9 0.8 multiply_bitcast_fusion
  20.8 0.7 iota_compare_fusion.5
  21.9 44.3 %all-to-all-done = f32[32,128,128]{2,1,0:T(8,128)} async-done(((f32[32,128,128]{2,1,0:T(8,128)}), f32[32,128,128]{2,1,0:T(8,128)}, u32[]{:S(2)}, u32[]{:S(2)}) %all-to-all-start) | async-done | bytes 2097184 | tf_op jit(solution)/shard_map/all_to_all | solution.py:99
  66.2 2.3 %gather_fusion = f32[32,128,128]{2,1,0:T(8,128)S(1)} fusion(f32[32,128,128]{2,1,0:T(8,128)} %all-to-all-done, s32[1024]{0:T(1024)S(1)} %pad_clamp_fusion.1), kind=kCustom, calls=%fused_computation | custom fusion | bytes 4194432 | tf_op jit(solution)/shard_map/gather | solution.py:100
  68.5 2.5 %fusion.12 = f32[32,128,128]{1,2,0:T(8,128)} fusion(f32[32,128,128]{2,1,0:T(8,128)S(1)} %gather_fusion, bf16[1,1,32,128,128]{4,3,2,1,0:T(8,128)(2,1)S(1)} %copy-done), kind=kOutput, calls=%fused_computation.19 | convolution fusion | flops 805306368 | bytes 5242880 | tf_op jit(solution)/shard_map/bld,bde->ble/dot_general | solution.py:10
  71.0 4.5 %fusion.1 = bf16[32,128,128]{2,1,0:T(8,128)(2,1)} fusion(f32[32,128,128]{1,2,0:T(8,128)} %fusion.12, bf16[1,1,32,128,128]{4,3,2,1,0:T(8,128)(2,1)} %param.10, bf16[1,1,32,128,128]{4,3,2,1,0:T(8,128)(2,1)} %param.9, bf16[1,1,32,128,128]{4,3,2,1,0:T(8,128)(2,1)S(1)} %copy-done, f32[32,128]{1,0:T(8,128)S(1)} %get-tuple-element.7, ...), kind=kOutput, calls=%fused_computation.9 | convolution fusion | flops 272629760 | bytes 6390016 | tf_op jit(solution)/shard_map/bij,bjd->bid/dot_general | solution.py:25
  75.6 1.2 broadcast_in_dim.47
  76.8 5.2 %scatter_fusion.1 = bf16[32,128,128]{2,1,0:T(8,128)(2,1)} fusion(bf16[32,128,128]{2,1,0:T(8,128)(2,1)} %broadcast_in_dim.47, s32[32]{0:T(128)S(1)} %fusion.23, bf16[32,128,128]{2,1,0:T(8,128)(2,1)} %fusion.1), kind=kCustom, calls=%fused_computation.5 | custom fusion | bytes 3145856 | tf_op jit(solution)/shard_map/scatter | solution.py:105
  82.0 4.3 %all-to-all-start.1 = ((bf16[32,128,128]{2,1,0:T(8,128)(2,1)}), bf16[32,128,128]{2,1,0:T(8,128)(2,1)}, u32[]{:S(2)}, u32[]{:S(2)}) async-start(bf16[32,128,128]{2,1,0:T(8,128)(2,1)} %scatter_fusion.1), calls=%async_computation.1 | async-start | bytes 2097152 | tf_op jit(solution)/shard_map/all_to_all | solution.py:109
  86.3 5.5 %multiply_add_fusion = f32[32,128,128]{2,1,0:T(8,128)} fusion(f32[32,128,128]{2,1,0:T(8,128)S(1)} %gather_fusion, bf16[1,1,32,128,128]{4,3,2,1,0:T(8,128)(2,1)} %param.10, bf16[1,1,32,128,128]{4,3,2,1,0:T(8,128)(2,1)} %param.9, f32[32,128]{1,0:T(8,128)S(1)} %get-tuple-element.6, f32[32]{0:T(128)S(1)} %get-tuple-element.4), kind=kOutput, calls=%fused_computation.13 | convolution fusion | flops 807403520 | bytes 6307968 | tf_op jit(solution)/shard_map/bjd,bje->bde/dot_general | solution.py:34
  91.8 1.6 broadcast_in_dim.53
  93.3 0.8 copy-done.1
  94.1 5.3 %scatter_fusion.2 = f32[32,128,128]{2,1,0:T(8,128)} fusion(f32[32,128,128]{2,1,0:T(8,128)} %broadcast_in_dim.53, s32[32]{0:T(128)S(1)} %fusion.23, f32[32,128,128]{2,1,0:T(8,128)S(1)} %copy-done.1), kind=kCustom, calls=%fused_computation.6 | custom fusion | bytes 6291584 | tf_op jit(solution)/shard_map/scatter | solution.py:107
  99.5 12.1 %all-to-all-done.1 = bf16[32,128,128]{2,1,0:T(8,128)(2,1)} async-done(((bf16[32,128,128]{2,1,0:T(8,128)(2,1)}), bf16[32,128,128]{2,1,0:T(8,128)(2,1)}, u32[]{:S(2)}, u32[]{:S(2)}) %all-to-all-start.1) | async-done | bytes 1048608 | tf_op jit(solution)/shard_map/all_to_all | solution.py:109
  111.6 3.6 %all-to-all-start.2 = ((f32[32,128,128]{2,1,0:T(8,128)}), f32[32,128,128]{2,1,0:T(8,128)S(1)}, u32[]{:S(2)}, u32[]{:S(2)}) async-start(f32[32,128,128]{2,1,0:T(8,128)} %scatter_fusion.2), calls=%async_computation.2 | async-start | bytes 4194304 | tf_op jit(solution)/shard_map/all_to_all | solution.py:112
  115.2 2.9 %gather_fusion.1 = bf16[32,128,128]{2,1,0:T(8,128)(2,1)} fusion(bf16[32,128,128]{2,1,0:T(8,128)(2,1)} %all-to-all-done.1, s32[1024]{0:T(1024)S(1)} %pad_clamp_fusion), kind=kCustom, calls=%fused_computation.1 | custom fusion | bytes 2097280 | tf_op jit(solution)/shard_map/gather | solution.py:114
  118.1 44.8 %all-to-all-done.2 = f32[32,128,128]{2,1,0:T(8,128)S(1)} async-done(((f32[32,128,128]{2,1,0:T(8,128)}), f32[32,128,128]{2,1,0:T(8,128)S(1)}, u32[]{:S(2)}, u32[]{:S(2)}) %all-to-all-start.2) | async-done | bytes 2097184 | tf_op jit(solution)/shard_map/all_to_all | solution.py:112
  162.9 2.0 %gather_fusion.2 = f32[32,128,128]{2,1,0:T(8,128)} fusion(f32[32,128,128]{2,1,0:T(8,128)S(1)} %all-to-all-done.2, s32[1024]{0:T(1024)S(1)} %pad_clamp_fusion), kind=kCustom, calls=%fused_computation.2 | custom fusion | bytes 4194432 | tf_op jit(solution)/shard_map/gather | solution.py:115
  (36 shorter events, 2.7 us)
Async XLA Ops:
  0.6 67.9 %copy-start = (bf16[1,1,32,128,128]{4,3,2,1,0:T(8,128)(2,1)S(1)}, bf16[1,1,32,128,128]{4,3,2,1,0:T(8,128)(2,1)}, u32[]{:S(2)}) copy-start(bf16[1,1,32,128,128]{4,3,2,1,0:T(8,128)(2,1)} %param.8) | copy-start | bytes 3145732
  0.6 5.5 %copy-start.2 = (f32[1,1,32,128,128]{4,3,2,1,0:T(8,128)S(1)}, f32[1,1,32,128,128]{4,3,2,1,0:T(8,128)}, u32[]{:S(2)}) copy-start(f32[1,1,32,128,128]{4,3,2,1,0:T(8,128)} %param.11) | copy-start | bytes 6291460
  11.5 7.4 %copy-start.3 = (s32[4]{0:T(128)S(1)}, s32[4]{0:T(128)}, u32[]{:S(2)}) copy-start(s32[4]{0:T(128)} %param.12) | copy-start | bytes 52
  11.5 10.1 %copy-start.4 = (f32[64]{0:T(128)S(1)}, f32[64]{0:T(128)}, u32[]{:S(2)}) copy-start(f32[64]{0:T(128)} %param.15) | copy-start | bytes 772
  11.5 10.1 %copy-start.5 = (s32[1,32]{1,0:T(1,128)S(1)}, s32[1,32]{1,0:T(1,128)}, u32[]{:S(2)}) copy-start(s32[1,32]{1,0:T(1,128)} %param.14) | copy-start | bytes 388
  11.5 54.8 %all-to-all-start = ((f32[32,128,128]{2,1,0:T(8,128)}), f32[32,128,128]{2,1,0:T(8,128)}, u32[]{:S(2)}, u32[]{:S(2)}) async-start(f32[32,128,128]{2,1,0:T(8,128)} %scatter_fusion), calls=%async_computation | async-start | bytes 4194304 | tf_op jit(solution)/shard_map/all_to_all | solution.py:99
  82.0 29.6 %all-to-all-start.1 = ((bf16[32,128,128]{2,1,0:T(8,128)(2,1)}), bf16[32,128,128]{2,1,0:T(8,128)(2,1)}, u32[]{:S(2)}, u32[]{:S(2)}) async-start(bf16[32,128,128]{2,1,0:T(8,128)(2,1)} %scatter_fusion.1), calls=%async_computation.1 | async-start | bytes 2097152 | tf_op jit(solution)/shard_map/all_to_all | solution.py:109
  91.8 2.3 %copy-start.1 = (f32[32,128,128]{2,1,0:T(8,128)S(1)}, f32[32,128,128]{2,1,0:T(8,128)}, u32[]{:S(2)}) copy-start(f32[32,128,128]{2,1,0:T(8,128)} %multiply_add_fusion) | copy-start | bytes 6291460
  111.6 51.3 %all-to-all-start.2 = ((f32[32,128,128]{2,1,0:T(8,128)}), f32[32,128,128]{2,1,0:T(8,128)S(1)}, u32[]{:S(2)}, u32[]{:S(2)}) async-start(f32[32,128,128]{2,1,0:T(8,128)} %scatter_fusion.2), calls=%async_computation.2 | async-start | bytes 4194304 | tf_op jit(solution)/shard_map/all_to_all | solution.py:112
where the time goes:
time: 166 us; the launch traced here: 165 us
  waiting for transfers between devices  101 us (61%)
  local copies, waits for them, and re-layouts  29.1 us (18%)
  starting transfers between devices  14.3 us (9%)
  matrix products  12.5 us (8%)
  other arithmetic  5.54 us (3%)
  between operations  2.09 us (1%)
    all_to_all x1, waiting for transfers between devices, local(): lax.all_to_all(finals_send, 'replica', split_axis=0, concat_axis=0, tiled...  44.8 us
    all_to_all x1, waiting for transfers between devices, local(): lax.all_to_all(state_send, 'replica', split_axis=0, concat_axis=0, tiled=...  44.3 us
    all_to_all x1, waiting for transfers between devices, local(): lax.all_to_all(rows_send.astype(jnp.float32), 'replica', split_axis=0, co...  12.1 us
    all_to_all x1, starting transfers between devices, local(): lax.all_to_all(state_send, 'replica', split_axis=0, concat_axis=0, tiled=...  6.45 us
    dot_general x1, matrix products, delta_part(): jnp.einsum('bjd,bje->bde', scaled, value_block.astype(jnp.float32), preci...  5.47 us
    scatter x1, local copies, waits for them, and re-layouts, local(): jnp.zeros((slot_total, head_size, head_size), jnp.float32).at[chosen]  5.32 us
    scatter x1, local copies, waits for them, and re-layouts, local(): jnp.zeros((slot_total, head_size, head_size), jnp.float32).at[position]  5.32 us
    scatter x1, local copies, waits for them, and re-layouts, local(): jnp.zeros((slot_total, token_slots, head_size), jnp.bfloat16).at[position]  5.24 us
  transfers between devices with their start and end apart: 3, of which 3 were waited for; matrix products, arithmetic and copies ran while one was open for 11% of the time, Pallas kernels for 0%

commit v1 on v0

v1 whole, which is shorter than its diff:
```python
import functools

import jax
import jax.numpy as jnp
from jax import lax
from jax.experimental import pallas as pl
from jax.experimental.pallas import tpu as pltpu
from jax.sharding import PartitionSpec as P

MESH = pl.DeviceIdType.MESH


def item(query, key, value, state, rate, count, gaps, rows):
    size = state.shape[1]
    scores = lax.dot_general(
        query, key, (((1,), (1,)), ((), ())), preferred_element_type=jnp.float32
    )
    weight = jnp.where(gaps >= 0.0, jnp.exp(-rate * jnp.maximum(gaps, 0.0)), 0.0)
    probs = (scores * weight).astype(jnp.bfloat16)
    intra = jnp.dot(probs, value, preferred_element_type=jnp.float32)
    high = state.astype(jnp.bfloat16)
    low = (state - high.astype(jnp.float32)).astype(jnp.bfloat16)
    mixed = jnp.dot(
        query, jnp.concatenate([high, low], axis=1), preferred_element_type=jnp.float32
    )
    mixed = mixed[:, :size] + mixed[:, size:]
    powers = jnp.exp(-rate * (rows.astype(jnp.float32) + 1.0))
    result = jnp.where(rows < count, intra + powers * mixed, 0.0).astype(jnp.bfloat16)
    remain = jnp.maximum(count - 1 - rows, 0).astype(jnp.float32)
    fade = jnp.where(rows < count, jnp.exp(-rate * remain), 0.0)
    scaled = value.astype(jnp.float32) * fade
    high = scaled.astype(jnp.bfloat16)
    low = (scaled - high.astype(jnp.float32)).astype(jnp.bfloat16)
    delta = lax.dot_general(
        key,
        jnp.concatenate([high, low], axis=1),
        (((0,), (0,)), ((), ())),
        preferred_element_type=jnp.float32,
    )
    delta = delta[:, :size] + delta[:, size:]
    kept = jnp.exp(jnp.full((1, size), -rate * count.astype(jnp.float32)))
    return result, kept * state + delta


def kernel(
    replicas, per_pair, full,
    order_ref, chosen_ref, rate_ref, count_ref, q_ref, k_ref, v_ref, state_hbm,
    rows_hbm, final_hbm,
    send, recv, state_ref, rows_ref, final_ref,
    state_sem, send_sem, recv_sem, rows_sem, final_sem,
):
    heads, tokens = q_ref.shape[0], q_ref.shape[1]
    me = lax.axis_index("replica")

    barrier = pltpu.get_barrier_semaphore()
    for step in range(1, replicas):
        pl.semaphore_signal(
            barrier, inc=1, device_id={"replica": lax.rem(me + step, replicas)},
            device_id_type=MESH,
        )
    state_copy = pltpu.make_async_copy(state_hbm, state_ref, state_sem)
    state_copy.start()

    def stage(target, buffer, place):
        head = order_ref[target]
        buffer[place, 0] = q_ref[head]
        buffer[place, 1] = k_ref[head]
        buffer[place, 2] = v_ref[head]

    def outgoing(step, rank):
        return pltpu.make_async_remote_copy(
            src_ref=send.at[step * per_pair + rank],
            dst_ref=recv.at[me * per_pair + rank],
            send_sem=send_sem.at[step * per_pair + rank],
            recv_sem=recv_sem.at[me * per_pair + rank],
            device_id={"replica": lax.rem(me + step, replicas)},
            device_id_type=MESH,
        )

    for rank in range(per_pair):
        for step in range(1, replicas):
            target = lax.rem(me + step, replicas)
            stage(target * per_pair + rank, send, step * per_pair + rank)
            if rank == 0 and step == 1:
                pl.semaphore_wait(barrier, replicas - 1)
            outgoing(step, rank).start()

    def stage_own(rank, carry):
        stage(me * per_pair + rank, recv, me * per_pair + rank)
        return carry

    lax.fori_loop(0, per_pair, stage_own, 0)

    across = lax.broadcasted_iota(jnp.int32, (tokens, tokens), 1)
    down = lax.broadcasted_iota(jnp.int32, (tokens, tokens), 0)
    gaps = (down - across).astype(jnp.float32)
    rows = lax.broadcasted_iota(jnp.int32, (tokens, q_ref.shape[2]), 0)

    def out_copies(slot):
        return (
            pltpu.make_async_copy(rows_ref.at[slot], rows_hbm.at[slot], rows_sem.at[slot]),
            pltpu.make_async_copy(final_ref.at[slot], final_hbm.at[slot], final_sem.at[slot]),
        )

    def compute(slot, block):
        result, final = item(
            recv[block, 0], recv[block, 1], recv[block, 2], state_ref[slot],
            rate_ref[slot], count_ref[slot], gaps, rows,
        )
        rows_ref[slot] = result
        final_ref[slot] = final
        for copy in out_copies(slot):
            copy.start()

    def arrived(block):
        pltpu.make_async_copy(recv.at[block], recv.at[block], recv_sem.at[block]).wait()

    state_copy.wait()
    if full:

        def own(rank, carry):
            slot = me * per_pair + rank
            compute(slot, slot)
            return carry

        lax.fori_loop(0, per_pair, own, 0)

        def others(rank, carry):
            for step in range(1, replicas):
                slot = lax.rem(me + replicas - step, replicas) * per_pair + rank
                arrived(slot)
                compute(slot, slot)
            return carry

        lax.fori_loop(0, per_pair, others, 0)
    else:
        for rank in range(per_pair):
            for step in range(1, replicas):
                arrived(lax.rem(me + step, replicas) * per_pair + rank)

        def each(slot, carry):
            compute(slot, chosen_ref[slot])
            return carry

        lax.fori_loop(0, heads, each, 0)

    for rank in range(per_pair):
        for step in range(1, replicas):
            outgoing(step, rank).wait_send()

    def drain(slot, carry):
        for copy in out_copies(slot):
            copy.wait()
        return carry

    lax.fori_loop(0, heads, drain, 0)


def local(queries, key_rows, value_rows, state_in, lengths, assignment, head_rate, decay_table):
    query_rows, key_block, value_block = queries[0, 0], key_rows[0, 0], value_rows[0, 0]
    held_state = state_in[0, 0]
    heads, tokens, size = query_rows.shape
    replicas = lax.axis_size("replica")
    per_pair = max(1, heads // replicas)
    slots = replicas * per_pair
    full = slots == heads
    myself = lax.axis_index("replica")
    my_layer = lax.axis_index("section")
    my_block = lax.axis_index("tensor")
    targets = lax.dynamic_slice(
        assignment, (jnp.int32(0), my_layer, my_block * heads), (replicas, 1, heads)
    )[:, 0, :]
    number = jnp.arange(heads, dtype=jnp.int32)
    earlier = number[None, :] < number[:, None]
    own = lax.dynamic_index_in_dim(targets, myself, 0, keepdims=False)
    own_rank = jnp.sum((own[:, None] == own[None, :]) & earlier, axis=1, dtype=jnp.int32)
    place = own * per_pair + own_rank
    order = jnp.sum(
        jnp.where(place[None, :] == jnp.arange(slots)[:, None], number[None, :], 0),
        axis=1, dtype=jnp.int32,
    )
    mine = targets == myself
    rank = jnp.sum(mine[:, None, :] & earlier[None], axis=2, dtype=jnp.int32)
    hit = mine[:, None, :] & (rank[:, None, :] == jnp.arange(per_pair)[None, :, None])
    hit = hit.reshape(slots, heads)
    picks = head_rate[0][:, None] == jnp.arange(decay_table.shape[0])[None, :]
    head_decay = jnp.sum(jnp.where(picks, decay_table[None, :], 0.0), axis=1)
    rates = jnp.sum(jnp.where(hit, head_decay[None, :], 0.0), axis=1)
    counts = jnp.repeat(lengths, per_pair)
    if full:
        chosen = jnp.zeros((1,), jnp.int32)
    else:
        taken = jnp.any(hit, axis=1)
        before = jnp.cumsum(taken.astype(jnp.int32)) - 1
        spot = taken[None, :] & (before[None, :] == number[:, None])
        chosen = jnp.sum(
            jnp.where(spot, jnp.arange(slots, dtype=jnp.int32)[None, :], 0),
            axis=1, dtype=jnp.int32,
        )
        rates = jnp.sum(jnp.where(spot, rates[None, :], 0.0), axis=1)
        counts = jnp.sum(jnp.where(spot, counts[None, :], 0), axis=1, dtype=jnp.int32)
    smem = pl.BlockSpec(memory_space=pltpu.SMEM)
    vmem = pl.BlockSpec(memory_space=pltpu.VMEM)
    anywhere = pl.BlockSpec(memory_space=pl.ANY)
    rows_out, final_out = pl.pallas_call(
        functools.partial(kernel, replicas, per_pair, full),
        out_shape=(
            jax.ShapeDtypeStruct((heads, tokens, size), jnp.bfloat16),
            jax.ShapeDtypeStruct((heads, size, size), jnp.float32),
        ),
        in_specs=[smem] * 4 + [vmem] * 3 + [anywhere],
        out_specs=(anywhere, anywhere),
        scratch_shapes=[
            pltpu.VMEM((slots, 3, tokens, size), jnp.bfloat16),
            pltpu.VMEM((slots, 3, tokens, size), jnp.bfloat16),
            pltpu.VMEM((heads, size, size), jnp.float32),
            pltpu.VMEM((heads, tokens, size), jnp.bfloat16),
            pltpu.VMEM((heads, size, size), jnp.float32),
            pltpu.SemaphoreType.DMA,
            pltpu.SemaphoreType.DMA((slots,)),
            pltpu.SemaphoreType.DMA((slots,)),
            pltpu.SemaphoreType.DMA((heads,)),
            pltpu.SemaphoreType.DMA((heads,)),
        ],
        compiler_params=pltpu.CompilerParams(
            collective_id=0, has_side_effects=True, vmem_limit_bytes=24 * 1024 * 1024
        ),
    )(order, chosen, rates, counts, query_rows, key_block, value_block, held_state)
    return (rows_out[None, None], final_out[None, None])


def solution(mesh):
    in_specs = (
        P(("groups", "replica"), "section", "tensor", None, None),
        P(("groups", "replica"), "section", "tensor", None, None),
        P(("groups", "replica"), "section", "tensor", None, None),
        P(("groups", "replica"), "section", "tensor", None, None),
        P("groups"),
        P("groups", None, None),
        P("section", "tensor"),
        P(),
    )
    out_specs = (
        P(("groups", "replica"), "section", "tensor", None, None),
        P(("groups", "replica"), "section", "tensor", None, None),
    )
    return jax.shard_map(local, mesh=mesh, in_specs=in_specs, out_specs=out_specs, check_vma=False)
```

time: 166 us -> 87.4 us (0.53)
  waiting for transfers between devices: 101 us -> 0 us
  Pallas kernels: 0 us -> 74.2 us
  local copies, waits for them, and re-layouts: 29.1 us -> 9.23 us
  starting transfers between devices: 14.3 us -> 0 us
  matrix products: 12.5 us -> 0 us
  other arithmetic: 5.54 us -> 2.92 us
    all_to_all x3 -> x0, waiting for transfers between devices: 101 us -> none  [the longest x1 44.8 us: local(): lax.all_to_all(finals_send, 'replica', split_axis=0, concat_axis=0, tiled...]
    pallas_call x0 -> x1, Pallas kernels: none -> 74.2 us  [local(): pl.pallas_call(functools.partial(kernel, replicas, per_pair, full), out_s...]
    scatter x3 -> x0, local copies, waits for them, and re-layouts: 15.9 us -> none  [the longest x1 5.32 us: local(): jnp.zeros((slot_total, head_size, head_size), jnp.float32).at[chosen]]
    all_to_all x3 -> x0, starting transfers between devices: 14.3 us -> none  [the longest x1 6.45 us: local(): lax.all_to_all(state_send, 'replica', split_axis=0, concat_axis=0, tiled=...]
    dot_general x3 -> x0, matrix products: 12.5 us -> none  [the longest x1 5.47 us: delta_part(): jnp.einsum('bjd,bje->bde', scaled, value_block.astype(jnp.float32), preci...]
    gather x3 -> x0, local copies, waits for them, and re-layouts: 7.14 us -> none  [the longest x1 2.87 us: local(): helper_rows = rows_back[chosen]]
    unnamed x13 -> x11, local copies, waits for them, and re-layouts: 0.82 us -> 7.57 us
    broadcast_in_dim x4 -> x1, local copies, waits for them, and re-layouts: 4.34 us -> 0.73 us  [local(): counts = jnp.repeat(lengths, per_pair)]
  transfers between devices with their start and end apart: 3 -> 0, of which waited for: 3 -> 0; matrix products, arithmetic and copies ran while one was open for 11% -> 0% of each run, Pallas kernels for 0% -> 0%
where the time goes in v1:
time: 87.4 us; the launch traced here: 87 us
  Pallas kernels  74.2 us (85%)
  local copies, waits for them, and re-layouts  9.23 us (11%)
  other arithmetic  2.92 us (3%)
    pallas_call x1, Pallas kernels, local(): pl.pallas_call(functools.partial(kernel, replicas, per_pair, full), out_s...  74.2 us
    unnamed x11, local copies, waits for them, and re-layouts  7.57 us

profile of v1, /device:TPU:0, one launch (start us, length us, event | category | flops | bytes accessed | tf_op | source)
XLA Modules:
  0.0 87.0 jit_solution(12326314808716533400)
XLA Ops:
  0.6 0.9 select_reduce_fusion.1
  1.5 0.8 dynamic-slice_compare_fusion
  2.3 0.8 dynamic-slice_bitcast_fusion
  3.0 0.2 convert_reduce_fusion.1
  3.2 0.8 multiply_add_fusion
  4.0 0.1 select_reduce_fusion.2.order_ref
  4.1 0.7 broadcast_in_dim.63
  4.8 0.1 reshape.51.count_ref
  4.9 0.2 convert_reduce_fusion
  5.1 0.1 select_reduce_fusion
  5.2 0.1 reduce_sum.52.rate_ref
  5.3 0.0 copy-start
  5.3 1.6 %copy-done = f32[1,1,32,128,128]{4,3,2,1,0:T(8,128)S(1)} copy-done((f32[1,1,32,128,128]{4,3,2,1,0:T(8,128)S(1)}, f32[1,1,32,128,128]{4,3,2,1,0:T(8,128)}, u32[]{:S(2)}) %copy-start) | copy-done | bytes 2097176
  6.8 0.0 copy-start.1
  6.9 1.2 %copy-done.1 = bf16[1,1,32,128,128]{4,3,2,1,0:T(8,128)(2,1)S(1)} copy-done((bf16[1,1,32,128,128]{4,3,2,1,0:T(8,128)(2,1)S(1)}, bf16[1,1,32,128,128]{4,3,2,1,0:T(8,128)(2,1)}, u32[]{:S(2)}) %copy-start.1) | copy-done | bytes 1048600
  8.1 0.0 copy-start.2
  8.1 1.2 %copy-done.2 = bf16[1,1,32,128,128]{4,3,2,1,0:T(8,128)(2,1)S(1)} copy-done((bf16[1,1,32,128,128]{4,3,2,1,0:T(8,128)(2,1)S(1)}, bf16[1,1,32,128,128]{4,3,2,1,0:T(8,128)(2,1)}, u32[]{:S(2)}) %copy-start.2) | copy-done | bytes 1048600
  9.3 0.0 copy-start.3
  9.3 1.2 %copy-done.3 = bf16[1,1,32,128,128]{4,3,2,1,0:T(8,128)(2,1)S(1)} copy-done((bf16[1,1,32,128,128]{4,3,2,1,0:T(8,128)(2,1)S(1)}, bf16[1,1,32,128,128]{4,3,2,1,0:T(8,128)(2,1)}, u32[]{:S(2)}) %copy-start.3) | copy-done | bytes 1048600
  10.5 74.2 %shard_map.95 = (bf16[32,128,128]{2,1,0:T(8,128)(2,1)S(1)}, f32[32,128,128]{2,1,0:T(8,128)S(1)}) custom-call(s32[32]{0:T(128)S(1)} %select_reduce_fusion.2.order_ref, s32[1]{0:T(128)} %constant.46.clone.1.chosen_ref, f32[32]{0:T(128)S(1)} %reduce_sum.52.rate_ref, s32[32]{0:T(128)S(1)} %reshape.51.count_ref, bf16[32,128,128]{2,1,0:T(8,128)(2,1)S(1)} %bitcast.16, ...), custom_call_target="tpu_custom_call" | custom-call | tf_op jit(solution)/shard_map/pallas_call | solution.py:205
  84.7 1.0 %copy.15 = bf16[1,1,32,128,128]{4,3,2,1,0:T(8,128)(2,1)} copy(bf16[1,1,32,128,128]{4,3,2,1,0:T(8,128)(2,1)S(1)} %bitcast.19) | data formatting | bytes 2097152
  85.7 1.3 %copy.16 = f32[1,1,32,128,128]{4,3,2,1,0:T(8,128)} copy(f32[1,1,32,128,128]{4,3,2,1,0:T(8,128)S(1)} %bitcast.15) | data formatting | bytes 4194304
  (2 shorter events, 0.0 us)
Async XLA Ops:
  5.3 1.6 %copy-start = (f32[1,1,32,128,128]{4,3,2,1,0:T(8,128)S(1)}, f32[1,1,32,128,128]{4,3,2,1,0:T(8,128)}, u32[]{:S(2)}) copy-start(f32[1,1,32,128,128]{4,3,2,1,0:T(8,128)} %param.11) | copy-start | bytes 6291460
  6.8 1.2 %copy-start.1 = (bf16[1,1,32,128,128]{4,3,2,1,0:T(8,128)(2,1)S(1)}, bf16[1,1,32,128,128]{4,3,2,1,0:T(8,128)(2,1)}, u32[]{:S(2)}) copy-start(bf16[1,1,32,128,128]{4,3,2,1,0:T(8,128)(2,1)} %param.8) | copy-start | bytes 3145732
  8.1 1.2 %copy-start.2 = (bf16[1,1,32,128,128]{4,3,2,1,0:T(8,128)(2,1)S(1)}, bf16[1,1,32,128,128]{4,3,2,1,0:T(8,128)(2,1)}, u32[]{:S(2)}) copy-start(bf16[1,1,32,128,128]{4,3,2,1,0:T(8,128)(2,1)} %param.9) | copy-start | bytes 3145732
  9.3 1.2 %copy-start.3 = (bf16[1,1,32,128,128]{4,3,2,1,0:T(8,128)(2,1)S(1)}, bf16[1,1,32,128,128]{4,3,2,1,0:T(8,128)(2,1)}, u32[]{:S(2)}) copy-start(bf16[1,1,32,128,128]{4,3,2,1,0:T(8,128)(2,1)} %param.10) | copy-start | bytes 3145732

commit v2 on v1

--- a/solution.py
+++ b/solution.py
@@ -44,13 +44,16 @@
 
 def kernel(
     replicas, per_pair, full,
-    order_ref, chosen_ref, rate_ref, count_ref, q_ref, k_ref, v_ref, state_hbm,
+    asg_ref, length_ref, head_rate_ref, table_ref, q_hbm, k_hbm, v_hbm, state_hbm,
     rows_hbm, final_hbm,
-    send, recv, state_ref, rows_ref, final_ref,
-    state_sem, send_sem, recv_sem, rows_sem, final_sem,
+    q_ref, k_ref, v_ref, send, recv, state_ref, rows_ref, final_ref,
+    order_vmem, own_smem, order_smem,
+    load_sem, order_sem, send_sem, recv_sem, rows_sem, final_sem,
 ):
     heads, tokens = q_ref.shape[0], q_ref.shape[1]
     me = lax.axis_index("replica")
+    layer = lax.axis_index("section")
+    first = lax.axis_index("tensor") * heads
 
     barrier = pltpu.get_barrier_semaphore()
     for step in range(1, replicas):
@@ -58,11 +61,50 @@
             barrier, inc=1, device_id={"replica": lax.rem(me + step, replicas)},
             device_id_type=MESH,
         )
-    state_copy = pltpu.make_async_copy(state_hbm, state_ref, state_sem)
-    state_copy.start()
+    loads = [
+        pltpu.make_async_copy(source, target, load_sem.at[number])
+        for number, (source, target) in enumerate(
+            ((q_hbm, q_ref), (k_hbm, k_ref), (v_hbm, v_ref), (state_hbm, state_ref))
+        )
+    ]
+    for load in loads:
+        load.start()
+
+    width = asg_ref.shape[2]
+    lanes = order_vmem.shape[2]
+    layers = lax.broadcasted_iota(jnp.int32, (asg_ref.shape[1], width), 0)
+    col = lax.broadcasted_iota(jnp.int32, (width, width), 1)
+    row = lax.broadcasted_iota(jnp.int32, (width, width), 0)
+    inside = (row >= first) & (row < first + heads)
+    counted = (col >= first) & (col < row)
+    pair = lax.broadcasted_iota(jnp.int32, (width, lanes), 1)
+    head = lax.broadcasted_iota(jnp.int32, (width, lanes), 0) - first + 1
+
+    def find(replica):
+        named = jnp.sum(
+            jnp.where(layers == layer, asg_ref[replica], 0), axis=0, keepdims=True
+        )
+        along = jnp.broadcast_to(named, (width, width))
+        down = jnp.sum(jnp.where(row == col, along, 0), axis=1, keepdims=True)
+        rank = jnp.sum(
+            jnp.where(counted & (down == along), 1, 0), axis=1, keepdims=True
+        )
+        place = jnp.where(inside[:, :1], down * per_pair + rank, -1)
+        order_vmem[replica] = (
+            jnp.sum(jnp.where(place == pair, head, 0), axis=0, keepdims=True) - 1
+        )
+
+    find(me)
+    own_copy = pltpu.make_async_copy(order_vmem.at[me], own_smem, order_sem.at[0])
+    own_copy.start()
+    for load in loads[:3]:
+        load.wait()
+    own_copy.wait()
 
     def stage(target, buffer, place):
-        head = order_ref[target]
+        head = own_smem[0, target]
+        if not full:
+            head = jnp.maximum(head, 0)
         buffer[place, 0] = q_ref[head]
         buffer[place, 1] = k_ref[head]
         buffer[place, 2] = v_ref[head]
@@ -85,6 +127,14 @@
                 pl.semaphore_wait(barrier, replicas - 1)
             outgoing(step, rank).start()
 
+    def find_other(step, carry):
+        find(lax.rem(me + step, replicas))
+        return carry
+
+    lax.fori_loop(1, replicas, find_other, 0)
+    order_copy = pltpu.make_async_copy(order_vmem, order_smem, order_sem.at[1])
+    order_copy.start()
+
     def stage_own(rank, carry):
         stage(me * per_pair + rank, recv, me * per_pair + rank)
         return carry
@@ -102,10 +152,12 @@
             pltpu.make_async_copy(final_ref.at[slot], final_hbm.at[slot], final_sem.at[slot]),
         )
 
-    def compute(slot, block):
+    def compute(slot, source, rank):
+        block = source * per_pair + rank
+        head = jnp.maximum(order_smem[source, 0, me * per_pair + rank], 0)
         result, final = item(
             recv[block, 0], recv[block, 1], recv[block, 2], state_ref[slot],
-            rate_ref[slot], count_ref[slot], gaps, rows,
+            table_ref[head_rate_ref[0, head]], length_ref[source], gaps, rows,
         )
         rows_ref[slot] = result
         final_ref[slot] = final
@@ -115,21 +167,21 @@
     def arrived(block):
         pltpu.make_async_copy(recv.at[block], recv.at[block], recv_sem.at[block]).wait()
 
-    state_copy.wait()
+    loads[3].wait()
+    order_copy.wait()
     if full:
 
         def own(rank, carry):
-            slot = me * per_pair + rank
-            compute(slot, slot)
+            compute(me * per_pair + rank, me, rank)
             return carry
 
         lax.fori_loop(0, per_pair, own, 0)
 
         def others(rank, carry):
             for step in range(1, replicas):
-                slot = lax.rem(me + replicas - step, replicas) * per_pair + rank
-                arrived(slot)
-                compute(slot, slot)
+                source = lax.rem(me + replicas - step, replicas)
+                arrived(source * per_pair + rank)
+                compute(source * per_pair + rank, source, rank)
             return carry
 
         lax.fori_loop(0, per_pair, others, 0)
@@ -139,7 +191,16 @@
                 arrived(lax.rem(me + step, replicas) * per_pair + rank)
 
         def each(slot, carry):
-            compute(slot, chosen_ref[slot])
+            def scan(block, found):
+                seen, chosen = found
+                taken = order_smem[block // per_pair, 0, me * per_pair + block % per_pair] >= 0
+                chosen = jnp.where(taken & (seen == slot), block, chosen)
+                return seen + jnp.where(taken, 1, 0), chosen
+
+            chosen = lax.fori_loop(
+                0, replicas * per_pair, scan, (jnp.int32(0), jnp.int32(0))
+            )[1]
+            compute(slot, chosen // per_pair, chosen % per_pair)
             return carry
 
         lax.fori_loop(0, heads, each, 0)
@@ -157,75 +218,48 @@
 
 
 def local(queries, key_rows, value_rows, state_in, lengths, assignment, head_rate, decay_table):
-    query_rows, key_block, value_block = queries[0, 0], key_rows[0, 0], value_rows[0, 0]
-    held_state = state_in[0, 0]
-    heads, tokens, size = query_rows.shape
+    heads, tokens, size = queries.shape[2:]
     replicas = lax.axis_size("replica")
     per_pair = max(1, heads // replicas)
     slots = replicas * per_pair
-    full = slots == heads
-    myself = lax.axis_index("replica")
-    my_layer = lax.axis_index("section")
-    my_block = lax.axis_index("tensor")
-    targets = lax.dynamic_slice(
-        assignment, (jnp.int32(0), my_layer, my_block * heads), (replicas, 1, heads)
-    )[:, 0, :]
-    number = jnp.arange(heads, dtype=jnp.int32)
-    earlier = number[None, :] < number[:, None]
-    own = lax.dynamic_index_in_dim(targets, myself, 0, keepdims=False)
-    own_rank = jnp.sum((own[:, None] == own[None, :]) & earlier, axis=1, dtype=jnp.int32)
-    place = own * per_pair + own_rank
-    order = jnp.sum(
-        jnp.where(place[None, :] == jnp.arange(slots)[:, None], number[None, :], 0),
-        axis=1, dtype=jnp.int32,
-    )
-    mine = targets == myself
-    rank = jnp.sum(mine[:, None, :] & earlier[None], axis=2, dtype=jnp.int32)
-    hit = mine[:, None, :] & (rank[:, None, :] == jnp.arange(per_pair)[None, :, None])
-    hit = hit.reshape(slots, heads)
-    picks = head_rate[0][:, None] == jnp.arange(decay_table.shape[0])[None, :]
-    head_decay = jnp.sum(jnp.where(picks, decay_table[None, :], 0.0), axis=1)
-    rates = jnp.sum(jnp.where(hit, head_decay[None, :], 0.0), axis=1)
-    counts = jnp.repeat(lengths, per_pair)
-    if full:
-        chosen = jnp.zeros((1,), jnp.int32)
-    else:
-        taken = jnp.any(hit, axis=1)
-        before = jnp.cumsum(taken.astype(jnp.int32)) - 1
-        spot = taken[None, :] & (before[None, :] == number[:, None])
-        chosen = jnp.sum(
-            jnp.where(spot, jnp.arange(slots, dtype=jnp.int32)[None, :], 0),
-            axis=1, dtype=jnp.int32,
-        )
-        rates = jnp.sum(jnp.where(spot, rates[None, :], 0.0), axis=1)
-        counts = jnp.sum(jnp.where(spot, counts[None, :], 0), axis=1, dtype=jnp.int32)
+    lanes = -(-slots // 128) * 128
     smem = pl.BlockSpec(memory_space=pltpu.SMEM)
     vmem = pl.BlockSpec(memory_space=pltpu.VMEM)
+    held = pl.BlockSpec(memory_space=pltpu.HBM)
     anywhere = pl.BlockSpec(memory_space=pl.ANY)
+    block = pltpu.VMEM((heads, tokens, size), jnp.bfloat16)
     rows_out, final_out = pl.pallas_call(
-        functools.partial(kernel, replicas, per_pair, full),
+        functools.partial(kernel, replicas, per_pair, slots == heads),
         out_shape=(
             jax.ShapeDtypeStruct((heads, tokens, size), jnp.bfloat16),
             jax.ShapeDtypeStruct((heads, size, size), jnp.float32),
         ),
-        in_specs=[smem] * 4 + [vmem] * 3 + [anywhere],
+        in_specs=[vmem] + [smem] * 3 + [held] * 4,
         out_specs=(anywhere, anywhere),
         scratch_shapes=[
+            block, block, block,
             pltpu.VMEM((slots, 3, tokens, size), jnp.bfloat16),
             pltpu.VMEM((slots, 3, tokens, size), jnp.bfloat16),
             pltpu.VMEM((heads, size, size), jnp.float32),
-            pltpu.VMEM((heads, tokens, size), jnp.bfloat16),
+            block,
             pltpu.VMEM((heads, size, size), jnp.float32),
-            pltpu.SemaphoreType.DMA,
+            pltpu.VMEM((replicas, 1, lanes), jnp.int32),
+            pltpu.SMEM((1, lanes), jnp.int32),
+            pltpu.SMEM((replicas, 1, lanes), jnp.int32),
+            pltpu.SemaphoreType.DMA((4,)),
+            pltpu.SemaphoreType.DMA((2,)),
             pltpu.SemaphoreType.DMA((slots,)),
             pltpu.SemaphoreType.DMA((slots,)),
             pltpu.SemaphoreType.DMA((heads,)),
             pltpu.SemaphoreType.DMA((heads,)),
         ],
         compiler_params=pltpu.CompilerParams(
-            collective_id=0, has_side_effects=True, vmem_limit_bytes=24 * 1024 * 1024
+            collective_id=0, has_side_effects=True, vmem_limit_bytes=56 * 1024 * 1024
         ),
-    )(order, chosen, rates, counts, query_rows, key_block, value_block, held_state)
+    )(
+        assignment, lengths, head_rate, decay_table,
+        queries[0, 0], key_rows[0, 0], value_rows[0, 0], state_in[0, 0],
+    )
     return (rows_out[None, None], final_out[None, None])
 
 

time: 87.4 us -> 80.8 us (0.924)
  local copies, waits for them, and re-layouts: 9.23 us -> 3.78 us
  other arithmetic: 2.92 us -> 0 us
  Pallas kernels: 74.2 us -> 76.2 us
    unnamed x11 -> x4, local copies, waits for them, and re-layouts: 7.57 us -> 3.78 us
    pallas_call x1, Pallas kernels: 74.2 us -> 76.2 us  [local(): pl.pallas_call(functools.partial(kernel, replicas, per_pair, slots == hea...]
    reduce_sum x5 -> x0, other arithmetic: 1.39 us -> none  [the longest x1 0.85 us: local(): head_decay = jnp.sum(jnp.where(picks, decay_table[None, :], 0.0), axis=1)]
where the time goes in v2:
time: 80.8 us; the launch traced here: 80.7 us
  Pallas kernels  76.2 us (94%)
  local copies, waits for them, and re-layouts  3.78 us (5%)
    pallas_call x1, Pallas kernels, local(): pl.pallas_call(functools.partial(kernel, replicas, per_pair, slots == hea...  76.2 us
    unnamed x4, local copies, waits for them, and re-layouts  3.78 us

profile of v2, /device:TPU:0, one launch (start us, length us, event | category | flops | bytes accessed | tf_op | source)
XLA Modules:
  0.0 80.7 jit_solution(15644727963659796965)
XLA Ops:
  0.6 76.2 %shard_map.95 = (bf16[32,128,128]{2,1,0:T(8,128)(2,1)}, f32[32,128,128]{2,1,0:T(8,128)}) custom-call(s32[4,2,64]{2,1,0:T(2,128)} %asg_ref.1, s32[4]{0:T(128)} %length_ref.1, s32[1,32]{1,0:T(1,128)} %head_rate_ref.1, f32[64]{0:T(128)} %table_ref.1, bf16[32,128,128]{2,1,0:T(8,128)(2,1)} %bitcast.9, bf16[32,128,128]{2,1,0:T(8,128)(2,1)} %bitcast.10, ...), custom_call_target="tpu_custom_call" | custom-call | tf_op jit(solution)/shard_map/pallas_call | solution.py:231
  76.9 0.0 copy-start
  76.9 2.5 %copy.12 = bf16[1,1,32,128,128]{4,3,2,1,0:T(8,128)(2,1)} copy(bf16[1,1,32,128,128]{4,3,2,1,0:T(8,128)(2,1)} %bitcast.8) | data formatting | bytes 2097152
  79.3 0.0 copy-done
  79.3 1.3 %copy.13 = f32[1,1,32,128,128]{4,3,2,1,0:T(8,128)} copy(f32[1,1,32,128,128]{4,3,2,1,0:T(8,128)S(1)} %bitcast.6) | data formatting | bytes 4194304
Async XLA Ops:
  76.9 2.5 %copy-start = (f32[32,128,128]{2,1,0:T(8,128)S(1)}, f32[32,128,128]{2,1,0:T(8,128)}, u32[]{:S(2)}) copy-start(f32[32,128,128]{2,1,0:T(8,128)} %get-tuple-element.5) | copy-start | bytes 6291460

commit v3 on v2

--- a/solution.py
+++ b/solution.py
@@ -45,15 +45,28 @@
 def kernel(
     replicas, per_pair, full,
     asg_ref, length_ref, head_rate_ref, table_ref, q_hbm, k_hbm, v_hbm, state_hbm,
-    rows_hbm, final_hbm,
-    q_ref, k_ref, v_ref, send, recv, state_ref, rows_ref, final_ref,
+    rows_ref, final_ref,
+    q_ref, k_ref, v_ref, send, recv, state_ref,
     order_vmem, own_smem, order_smem,
-    load_sem, order_sem, send_sem, recv_sem, rows_sem, final_sem,
+    load_sem, order_sem, send_sem, recv_sem,
 ):
     heads, tokens = q_ref.shape[0], q_ref.shape[1]
     me = lax.axis_index("replica")
     layer = lax.axis_index("section")
     first = lax.axis_index("tensor") * heads
+
+    half = replicas // 2
+    side, spot = me // half, me % half
+
+    def receiver(step):
+        if step <= half:
+            return (1 - side) * half + (spot + step - 1) % half
+        return side * half + (spot + step - half) % half
+
+    def sender(step):
+        if step <= half:
+            return (1 - side) * half + (spot + half - (step - 1)) % half
+        return side * half + (spot + half - (step - half)) % half
 
     barrier = pltpu.get_barrier_semaphore()
     for step in range(1, replicas):
@@ -115,13 +128,13 @@
             dst_ref=recv.at[me * per_pair + rank],
             send_sem=send_sem.at[step * per_pair + rank],
             recv_sem=recv_sem.at[me * per_pair + rank],
-            device_id={"replica": lax.rem(me + step, replicas)},
+            device_id={"replica": receiver(step)},
             device_id_type=MESH,
         )
 
     for rank in range(per_pair):
         for step in range(1, replicas):
-            target = lax.rem(me + step, replicas)
+            target = receiver(step)
             stage(target * per_pair + rank, send, step * per_pair + rank)
             if rank == 0 and step == 1:
                 pl.semaphore_wait(barrier, replicas - 1)
@@ -146,23 +159,18 @@
     gaps = (down - across).astype(jnp.float32)
     rows = lax.broadcasted_iota(jnp.int32, (tokens, q_ref.shape[2]), 0)
 
-    def out_copies(slot):
-        return (
-            pltpu.make_async_copy(rows_ref.at[slot], rows_hbm.at[slot], rows_sem.at[slot]),
-            pltpu.make_async_copy(final_ref.at[slot], final_hbm.at[slot], final_sem.at[slot]),
-        )
-
-    def compute(slot, source, rank):
-        block = source * per_pair + rank
-        head = jnp.maximum(order_smem[source, 0, me * per_pair + rank], 0)
-        result, final = item(
-            recv[block, 0], recv[block, 1], recv[block, 2], state_ref[slot],
-            table_ref[head_rate_ref[0, head]], length_ref[source], gaps, rows,
-        )
-        rows_ref[slot] = result
-        final_ref[slot] = final
-        for copy in out_copies(slot):
-            copy.start()
+    def compute(work):
+        done = []
+        for slot, source, rank in work:
+            block = source * per_pair + rank
+            head = jnp.maximum(order_smem[source, 0, me * per_pair + rank], 0)
+            done.append(item(
+                recv[block, 0], recv[block, 1], recv[block, 2], state_ref[slot],
+                table_ref[head_rate_ref[0, head]], length_ref[source], gaps, rows,
+            ))
+        for (slot, _, _), (result, final) in zip(work, done):
+            rows_ref[slot] = result
+            final_ref[slot] = final
 
     def arrived(block):
         pltpu.make_async_copy(recv.at[block], recv.at[block], recv_sem.at[block]).wait()
@@ -172,16 +180,16 @@
     if full:
 
         def own(rank, carry):
-            compute(me * per_pair + rank, me, rank)
+            compute([(me * per_pair + rank, me, rank)])
             return carry
 
         lax.fori_loop(0, per_pair, own, 0)
 
         def others(rank, carry):
-            for step in range(1, replicas):
-                source = lax.rem(me + replicas - step, replicas)
+            sources = [sender(step) for step in range(1, replicas)]
+            for source in sources:
                 arrived(source * per_pair + rank)
-                compute(source * per_pair + rank, source, rank)
+            compute([(source * per_pair + rank, source, rank) for source in sources])
             return carry
 
         lax.fori_loop(0, per_pair, others, 0)
@@ -200,7 +208,7 @@
             chosen = lax.fori_loop(
                 0, replicas * per_pair, scan, (jnp.int32(0), jnp.int32(0))
             )[1]
-            compute(slot, chosen // per_pair, chosen % per_pair)
+            compute([(slot, chosen // per_pair, chosen % per_pair)])
             return carry
 
         lax.fori_loop(0, heads, each, 0)
@@ -208,13 +216,6 @@
     for rank in range(per_pair):
         for step in range(1, replicas):
             outgoing(step, rank).wait_send()
-
-    def drain(slot, carry):
-        for copy in out_copies(slot):
-            copy.wait()
-        return carry
-
-    lax.fori_loop(0, heads, drain, 0)
 
 
 def local(queries, key_rows, value_rows, state_in, lengths, assignment, head_rate, decay_table):
@@ -226,22 +227,19 @@
     smem = pl.BlockSpec(memory_space=pltpu.SMEM)
     vmem = pl.BlockSpec(memory_space=pltpu.VMEM)
     held = pl.BlockSpec(memory_space=pltpu.HBM)
-    anywhere = pl.BlockSpec(memory_space=pl.ANY)
     block = pltpu.VMEM((heads, tokens, size), jnp.bfloat16)
     rows_out, final_out = pl.pallas_call(
         functools.partial(kernel, replicas, per_pair, slots == heads),
         out_shape=(
-            jax.ShapeDtypeStruct((heads, tokens, size), jnp.bfloat16),
-            jax.ShapeDtypeStruct((heads, size, size), jnp.float32),
+            pltpu.VMEM((heads, tokens, size), jnp.bfloat16),
+            pltpu.VMEM((heads, size, size), jnp.float32),
         ),
         in_specs=[vmem] + [smem] * 3 + [held] * 4,
-        out_specs=(anywhere, anywhere),
+        out_specs=(vmem, vmem),
         scratch_shapes=[
             block, block, block,
             pltpu.VMEM((slots, 3, tokens, size), jnp.bfloat16),
             pltpu.VMEM((slots, 3, tokens, size), jnp.bfloat16),
-            pltpu.VMEM((heads, size, size), jnp.float32),
-            block,
             pltpu.VMEM((heads, size, size), jnp.float32),
             pltpu.VMEM((replicas, 1, lanes), jnp.int32),
             pltpu.SMEM((1, lanes), jnp.int32),
@@ -250,11 +248,9 @@
             pltpu.SemaphoreType.DMA((2,)),
             pltpu.SemaphoreType.DMA((slots,)),
             pltpu.SemaphoreType.DMA((slots,)),
-            pltpu.SemaphoreType.DMA((heads,)),
-            pltpu.SemaphoreType.DMA((heads,)),
         ],
         compiler_params=pltpu.CompilerParams(
-            collective_id=0, has_side_effects=True, vmem_limit_bytes=56 * 1024 * 1024
+            collective_id=0, has_side_effects=True, vmem_limit_bytes=54 * 1024 * 1024
         ),
     )(
         assignment, lengths, head_rate, decay_table,

time: 80.8 us -> 78 us (0.965)
  local copies, waits for them, and re-layouts: 3.78 us -> 2.29 us
  Pallas kernels: 76.2 us -> 74.9 us
    unnamed x4 -> x2, local copies, waits for them, and re-layouts: 3.78 us -> 2.29 us
    pallas_call x1, Pallas kernels: 76.2 us -> 74.9 us  [local(): pl.pallas_call(functools.partial(kernel, replicas, per_pair, slots == hea...]
where the time goes in v3:
time: 78 us; the launch traced here: 77.8 us
  Pallas kernels  74.9 us (96%)
  local copies, waits for them, and re-layouts  2.29 us (3%)
    pallas_call x1, Pallas kernels, local(): pl.pallas_call(functools.partial(kernel, replicas, per_pair, slots == hea...  74.9 us
    unnamed x2, local copies, waits for them, and re-layouts  2.29 us

profile of v3, /device:TPU:0, one launch (start us, length us, event | category | flops | bytes accessed | tf_op | source)
XLA Modules:
  0.0 77.8 jit_solution(325304244725987863)
XLA Ops:
  0.6 74.9 %shard_map.95 = (bf16[32,128,128]{2,1,0:T(8,128)(2,1)S(1)}, f32[32,128,128]{2,1,0:T(8,128)S(1)}) custom-call(s32[4,2,64]{2,1,0:T(2,128)} %asg_ref.1, s32[4]{0:T(128)} %length_ref.1, s32[1,32]{1,0:T(1,128)} %head_rate_ref.1, f32[64]{0:T(128)} %table_ref.1, bf16[32,128,128]{2,1,0:T(8,128)(2,1)} %bitcast.9, bf16[32,128,128]{2,1,0:T(8,128)(2,1)} %bitcast.10, ...), custom_call_target="tpu_custom_call" | custom-call | tf_op jit(solution)/shard_map/pallas_call | solution.py:231
  75.5 1.0 %copy.12 = bf16[1,1,32,128,128]{4,3,2,1,0:T(8,128)(2,1)} copy(bf16[1,1,32,128,128]{4,3,2,1,0:T(8,128)(2,1)S(1)} %bitcast.7) | data formatting | bytes 2097152
  76.5 1.3 %copy.13 = f32[1,1,32,128,128]{4,3,2,1,0:T(8,128)} copy(f32[1,1,32,128,128]{4,3,2,1,0:T(8,128)S(1)} %bitcast.6) | data formatting | bytes 4194304

commit v4 on v3

--- a/solution.py
+++ b/solution.py
@@ -122,20 +122,23 @@
         buffer[place, 1] = k_ref[head]
         buffer[place, 2] = v_ref[head]
 
+    chunk = 2 if per_pair % 2 == 0 else 1
+
     def outgoing(step, rank):
         return pltpu.make_async_remote_copy(
-            src_ref=send.at[step * per_pair + rank],
-            dst_ref=recv.at[me * per_pair + rank],
+            src_ref=send.at[pl.ds(step * per_pair + rank, chunk)],
+            dst_ref=recv.at[pl.ds(me * per_pair + rank, chunk)],
             send_sem=send_sem.at[step * per_pair + rank],
             recv_sem=recv_sem.at[me * per_pair + rank],
             device_id={"replica": receiver(step)},
             device_id_type=MESH,
         )
 
-    for rank in range(per_pair):
+    for rank in range(0, per_pair, chunk):
         for step in range(1, replicas):
             target = receiver(step)
-            stage(target * per_pair + rank, send, step * per_pair + rank)
+            for one in range(rank, rank + chunk):
+                stage(target * per_pair + one, send, step * per_pair + one)
             if rank == 0 and step == 1:
                 pl.semaphore_wait(barrier, replicas - 1)
             outgoing(step, rank).start()
@@ -173,7 +176,8 @@
             final_ref[slot] = final
 
     def arrived(block):
-        pltpu.make_async_copy(recv.at[block], recv.at[block], recv_sem.at[block]).wait()
+        held = recv.at[pl.ds(block, chunk)]
+        pltpu.make_async_copy(held, held, recv_sem.at[block]).wait()
 
     loads[3].wait()
     order_copy.wait()
@@ -185,16 +189,18 @@
 
         lax.fori_loop(0, per_pair, own, 0)
 
-        def others(rank, carry):
+        def others(turn, carry):
             sources = [sender(step) for step in range(1, replicas)]
             for source in sources:
-                arrived(source * per_pair + rank)
-            compute([(source * per_pair + rank, source, rank) for source in sources])
+                arrived(source * per_pair + turn * chunk)
+            for one in range(chunk):
+                rank = turn * chunk + one
+                compute([(source * per_pair + rank, source, rank) for source in sources])
             return carry
 
-        lax.fori_loop(0, per_pair, others, 0)
+        lax.fori_loop(0, per_pair // chunk, others, 0)
     else:
-        for rank in range(per_pair):
+        for rank in range(0, per_pair, chunk):
             for step in range(1, replicas):
                 arrived(lax.rem(me + step, replicas) * per_pair + rank)
 
@@ -213,7 +219,7 @@
 
         lax.fori_loop(0, heads, each, 0)
 
-    for rank in range(per_pair):
+    for rank in range(0, per_pair, chunk):
         for step in range(1, replicas):
             outgoing(step, rank).wait_send()
 

time: 78 us -> 77 us (0.987); the launches traced: 77.8 us -> 76 us
  Pallas kernels: 74.9 us -> 73 us
    pallas_call x1, Pallas kernels: 74.9 us -> 73 us  [local(): pl.pallas_call(functools.partial(kernel, replicas, per_pair, slots == hea...]
where the time goes in v4:
time: 77 us; the launch traced here: 76 us
  Pallas kernels  73 us (95%)
  local copies, waits for them, and re-layouts  2.29 us (3%)
    pallas_call x1, Pallas kernels, local(): pl.pallas_call(functools.partial(kernel, replicas, per_pair, slots == hea...  73 us
    unnamed x2, local copies, waits for them, and re-layouts  2.29 us

profile of v4, /device:TPU:0, one launch (start us, length us, event | category | flops | bytes accessed | tf_op | source)
XLA Modules:
  0.0 76.0 jit_solution(5355978269600037697)
XLA Ops:
  0.6 73.0 %shard_map.95 = (bf16[32,128,128]{2,1,0:T(8,128)(2,1)S(1)}, f32[32,128,128]{2,1,0:T(8,128)S(1)}) custom-call(s32[4,2,64]{2,1,0:T(2,128)} %asg_ref.1, s32[4]{0:T(128)} %length_ref.1, s32[1,32]{1,0:T(1,128)} %head_rate_ref.1, f32[64]{0:T(128)} %table_ref.1, bf16[32,128,128]{2,1,0:T(8,128)(2,1)} %bitcast.9, bf16[32,128,128]{2,1,0:T(8,128)(2,1)} %bitcast.10, ...), custom_call_target="tpu_custom_call" | custom-call | tf_op jit(solution)/shard_map/pallas_call | solution.py:237
  73.7 1.0 %copy.12 = bf16[1,1,32,128,128]{4,3,2,1,0:T(8,128)(2,1)} copy(bf16[1,1,32,128,128]{4,3,2,1,0:T(8,128)(2,1)S(1)} %bitcast.7) | data formatting | bytes 2097152
  74.6 1.3 %copy.13 = f32[1,1,32,128,128]{4,3,2,1,0:T(8,128)} copy(f32[1,1,32,128,128]{4,3,2,1,0:T(8,128)S(1)} %bitcast.6) | data formatting | bytes 4194304

commit v5 on v4

--- a/solution.py
+++ b/solution.py
@@ -80,7 +80,7 @@
             ((q_hbm, q_ref), (k_hbm, k_ref), (v_hbm, v_ref), (state_hbm, state_ref))
         )
     ]
-    for load in loads:
+    for load in loads[:3]:
         load.start()
 
     width = asg_ref.shape[2]
@@ -142,6 +142,8 @@
             if rank == 0 and step == 1:
                 pl.semaphore_wait(barrier, replicas - 1)
             outgoing(step, rank).start()
+
+    loads[3].start()
 
     def find_other(step, carry):
         find(lax.rem(me + step, replicas))

time: 77 us -> 77.1 us (level)
  no operation moved by 1% of the time
where the time goes in v5:
time: 77.1 us; the launch traced here: 76 us
  Pallas kernels  73 us (95%)
  local copies, waits for them, and re-layouts  2.29 us (3%)
    pallas_call x1, Pallas kernels, local(): pl.pallas_call(functools.partial(kernel, replicas, per_pair, slots == hea...  73 us
    unnamed x2, local copies, waits for them, and re-layouts  2.29 us

profile of v5, /device:TPU:0, one launch (start us, length us, event | category | flops | bytes accessed | tf_op | source)
XLA Modules:
  0.0 76.0 jit_solution(13111571296305753445)
XLA Ops:
  0.6 73.0 %shard_map.95 = (bf16[32,128,128]{2,1,0:T(8,128)(2,1)S(1)}, f32[32,128,128]{2,1,0:T(8,128)S(1)}) custom-call(s32[4,2,64]{2,1,0:T(2,128)} %asg_ref.1, s32[4]{0:T(128)} %length_ref.1, s32[1,32]{1,0:T(1,128)} %head_rate_ref.1, f32[64]{0:T(128)} %table_ref.1, bf16[32,128,128]{2,1,0:T(8,128)(2,1)} %bitcast.9, bf16[32,128,128]{2,1,0:T(8,128)(2,1)} %bitcast.10, ...), custom_call_target="tpu_custom_call" | custom-call | tf_op jit(solution)/shard_map/pallas_call | solution.py:239
  73.7 1.0 %copy.12 = bf16[1,1,32,128,128]{4,3,2,1,0:T(8,128)(2,1)} copy(bf16[1,1,32,128,128]{4,3,2,1,0:T(8,128)(2,1)S(1)} %bitcast.7) | data formatting | bytes 2097152
  74.6 1.3 %copy.13 = f32[1,1,32,128,128]{4,3,2,1,0:T(8,128)} copy(f32[1,1,32,128,128]{4,3,2,1,0:T(8,128)S(1)} %bitcast.6) | data formatting | bytes 4194304
